TPU v7x, 32 devices: a whole 2x2x4 slice. The times are simulated.
32 devices in a mesh: term: 4 (over x, core), blk: 8 (over z, y).
Axes of the slice: x: 2, y: 2, z: 4, core: 2. Of those that a mesh axis runs over, the one named last changes fastest.
Arguments:
- wavefunction: bfloat16 [8, 8, 256, 256], P('blk'), may hold values from -6 to 6
- left_env: bfloat16 [8, 8, 256, 256], P('term', 'blk'), may hold values from -0.25 to 0.25
- right_env: bfloat16 [8, 8, 256, 256], P('term', 'blk'), may hold values from -0.25 to 0.25
- charges: int32 [8, 2], replicated, may hold values from 0 to 2
- sector_dims: int32 [8], replicated, may hold values from 192 to 256, as said below
Outputs:
- applied_once: bfloat16 [8, 8, 256, 256], P('term', 'blk')
- applied_twice: bfloat16 [8, 8, 256, 256], P('term', 'blk')
Inputs may be any that keep to these rules, and one draw needn't show every extreme that they name: `sector_dims`: some sector fills its tile.
All inputs are finite; a program needn't handle non-finite values.
Results may differ from a plain program's by a relative error of at most 0.017.
Values may be sent and summed in bfloat16 or wider, within the bound.
A program may use at most 64 MiB of HBM per device.

v0:
```python
import jax
import jax.numpy as jnp
from jax import lax
from jax.sharding import PartitionSpec as P


def allowed_pairs(charges):
    delta_n = charges[None, :, 0] - charges[:, None, 0]
    delta_s = charges[None, :, 1] - charges[:, None, 1]
    good = (jnp.abs(delta_n) <= 1) & (jnp.abs(delta_s) <= 1)
    return good.astype(jnp.float32)


def term_moves(term_count):
    first_term = lax.axis_index("term") * term_count
    return [(first_term + inner) % 3 - 1 for inner in range(term_count)]


def right_products(products, right_env):
    return jnp.einsum("wijac,wjdc->ijad", products, right_env, preferred_element_type=jnp.float32)


def apply_left_layout(vector_state, left_env, right_env, moves):
    products = jnp.einsum(
        "wiab,ijbc->wijac", left_env, vector_state, preferred_element_type=jnp.float32
    ).astype(jnp.bfloat16)
    rolled = jnp.stack(
        [jnp.roll(products[inner], -moves[inner], axis=1) for inner in range(len(moves))]
    )
    regrouped = lax.all_to_all(rolled, "blk", split_axis=2, concat_axis=1, tiled=True)
    placed = jnp.stack(
        [jnp.roll(regrouped[inner], moves[inner], axis=0) for inner in range(len(moves))]
    )
    return right_products(placed, right_env)


def on_device(wavefunction, left_env, right_env, charges, sector_dims):
    own_count = wavefunction.shape[0]
    tile_size = wavefunction.shape[2]
    moves = term_moves(left_env.shape[0])
    first_sector = lax.axis_index("blk") * own_count
    allowed = allowed_pairs(charges)
    live_rows = (jnp.arange(tile_size, dtype=jnp.int32)[None, :] < sector_dims[:, None]).astype(
        jnp.float32
    )
    mine_rows = lax.dynamic_slice_in_dim(live_rows, first_sector, own_count, 0)
    allowed_left = lax.dynamic_slice_in_dim(allowed, first_sector, own_count, 0)
    allowed_right = lax.dynamic_slice_in_dim(allowed, first_sector, own_count, 1)
    left_mask = (
        allowed_left[:, :, None, None] * mine_rows[:, None, :, None] * live_rows[None, :, None, :]
    )
    right_mask = (
        allowed_right[:, :, None, None] * live_rows[:, None, :, None] * mine_rows[None, :, None, :]
    )
    part_rows = right_mask.shape[0] // lax.axis_size("term")
    part_start = lax.axis_index("term") * part_rows
    slice_mask = lax.dynamic_slice_in_dim(right_mask, part_start, part_rows, 0)
    start = (wavefunction.astype(jnp.float32) * left_mask).astype(jnp.bfloat16)
    partial_value = apply_left_layout(start, left_env, right_env, moves)
    shared = lax.psum_scatter(
        partial_value.astype(jnp.bfloat16), "term", scatter_dimension=0, tiled=True
    ).astype(jnp.float32)
    applied_once = (shared * slice_mask).astype(jnp.bfloat16)
    full_next = lax.all_gather(applied_once, "term", axis=0, tiled=True)
    left_next = lax.all_to_all(full_next, "blk", split_axis=0, concat_axis=1, tiled=True)
    partial_next = apply_left_layout(left_next, left_env, right_env, moves)
    shared_next = lax.psum_scatter(
        partial_next.astype(jnp.bfloat16), "term", scatter_dimension=0, tiled=True
    ).astype(jnp.float32)
    applied_twice = (shared_next * slice_mask).astype(jnp.bfloat16)
    return (applied_once, applied_twice)


def solution(mesh):
    placed = (
        P("blk", None, None, None),
        P("term", "blk", None, None),
        P("term", "blk", None, None),
        P(),
        P(),
    )
    return jax.shard_map(
        on_device,
        mesh=mesh,
        in_specs=placed,
        out_specs=(P("term", "blk", None, None), P("term", "blk", None, None)),
        check_vma=False,
    )
```

profile of v0, /device:TPU:21, one launch (start us, length us, event | category | flops | bytes accessed | tf_op | source)
XLA Modules:
  0.0 236.9 jit_solution(2472696869790948133)
XLA Ops:
  7.2 0.0 copy-start
  7.3 0.8 slice_bitcast_fusion.9
  8.0 0.7 fusion.34
  8.7 0.1 fusion.37
  8.8 0.2 fusion.35
  9.0 0.1 broadcast_multiply_fusion
  9.1 0.0 copy-done
  9.1 2.3 convert_bitcast_fusion.1
  11.4 0.1 slice_bitcast_fusion.7
  11.6 0.8 fusion.19
  12.4 1.5 pad_maximum_fusion
  13.9 5.5 %all-to-all-start = ((bf16[2,1,8,256,256]{3,4,1,0,2:T(8,128)(2,1)}), bf16[2,1,8,256,256]{3,4,1,0,2:T(8,128)(2,1)S(1)}, u32[]{:S(2)}, u32[]{:S(2)}) async-start(bf16[2,1,8,256,256]{3,4,1,0,2:T(8,128)(2,1)} %pad_maximum_fusion), calls=%async_computation | async-start | bytes 4194304 | tf_op jit(solution)/shard_map/all_to_all | solution.py:30
  19.4 0.0 reduce-scatter.3.cloned.1.call-start
  19.4 44.7 %all-to-all-done = bf16[2,1,8,256,256]{3,4,1,0,2:T(8,128)(2,1)S(1)} async-done(((bf16[2,1,8,256,256]{3,4,1,0,2:T(8,128)(2,1)}), bf16[2,1,8,256,256]{3,4,1,0,2:T(8,128)(2,1)S(1)}, u32[]{:S(2)}, u32[]{:S(2)}) %all-to-all-start) | async-done | bytes 2097184 | tf_op jit(solution)/shard_map/all_to_all | solution.py:30
  64.2 0.1 slice_bitcast_fusion.5
  64.3 0.4 fusion.17
  64.7 0.5 copy.24
  65.3 0.4 fusion.16
  65.7 0.5 copy.25
  66.2 0.0 copy-start.1
  66.2 2.7 %fusion.6 = bf16[8,1,256,256]{3,2,0,1:T(8,128)(2,1)} fusion(bf16[1,8,1,256,256]{4,3,0,1,2:T(8,128)(2,1)S(1)} %bitcast.112, bf16[1,8,1,256,256]{4,3,0,1,2:T(8,128)(2,1)S(1)} %bitcast.111, bf16[2,1,256,256]{3,2,1,0:T(8,128)(2,1)} %param.11), kind=kOutput, calls=%fused_computation.31 | convolution fusion | flops 538443776 | bytes 3407872 | tf_op jit(solution)/shard_map/wijac,wjdc->ijad/dot_general | solution.py:20
  68.9 0.0 reduce-scatter.3.cloned.1.call-update
  68.9 0.0 all-gather.2.cloned.1.call-start
  69.0 0.0 copy-done.1
  69.0 0.1 fusion.33
  69.1 27.5 %reduce-scatter.3.cloned.1.call-done = bf16[2,1,256,256]{3,2,0,1:T(8,128)(2,1)} async-done(((bf16[8,1,256,256]{3,2,0,1:T(8,128)(2,1)}), bf16[2,1,256,256]{3,2,0,1:T(8,128)(2,1)}) %reduce-scatter.3.cloned.1.call-update) | async-done | bytes 262160 | tf_op jit(solution)/shard_map/reduce_scatter | solution.py:60
  96.6 1.8 fusion.27
  98.4 0.0 all-gather.2.cloned.1.call-update
  98.4 0.0 reduce-scatter.5.cloned.1.call-start
  98.4 17.5 %all-gather.2.cloned.1.call-done = bf16[8,1,256,256]{3,2,1,0:T(8,128)(2,1)} async-done(((bf16[2,1,256,256]{3,2,1,0:T(8,128)(2,1)}), bf16[8,1,256,256]{3,2,1,0:T(8,128)(2,1)}) %all-gather.2.cloned.1.call-update) | async-done | bytes 1048592 | tf_op jit(solution)/shard_map/all_gather | solution.py:64
  115.9 27.9 %all_to_all.12 = bf16[8,1,256,256]{3,2,1,0:T(8,128)(2,1)S(1)} all-to-all(bf16[8,1,256,256]{3,2,1,0:T(8,128)(2,1)} %all-gather.2.cloned.1.call-done), channel_id=1, replica_groups=mesh['term'=4,'blk'=8] {'blk'}, dimensions={0} | all-to-all | bytes 2097152 | tf_op jit(solution)/shard_map/all_to_all | solution.py:65
  143.9 0.8 convert_bitcast_fusion
  144.7 0.2 slice_bitcast_fusion.3
  144.8 0.4 fusion.15
  145.2 0.4 fusion.13
  145.6 0.2 pad_maximum_fusion.1
  145.8 51.4 %all_to_all.13 = bf16[2,1,8,256,256]{3,4,1,0,2:T(8,128)(2,1)S(1)} all-to-all(bf16[2,1,8,256,256]{3,4,1,0,2:T(8,128)(2,1)S(1)} %pad_maximum_fusion.1), channel_id=1, replica_groups=mesh['term'=4,'blk'=8] {'blk'}, dimensions={2} | all-to-all | bytes 4194304 | tf_op jit(solution)/shard_map/all_to_all | solution.py:30
  197.3 0.1 slice_bitcast_fusion.1
  197.4 0.4 fusion.11
  197.8 0.5 copy.28
  198.4 0.4 fusion.10
  198.8 0.5 copy.29
  199.3 2.7 %fusion.7 = bf16[8,1,256,256]{3,2,0,1:T(8,128)(2,1)} fusion(bf16[1,8,1,256,256]{4,3,0,1,2:T(8,128)(2,1)S(1)} %bitcast.113, bf16[1,8,1,256,256]{4,3,0,1,2:T(8,128)(2,1)S(1)} %bitcast.110, bf16[2,1,256,256]{3,2,1,0:T(8,128)(2,1)} %param.11), kind=kOutput, calls=%fused_computation.32 | convolution fusion | flops 538443776 | bytes 3407872 | tf_op jit(solution)/shard_map/wijac,wjdc->ijad/dot_general | solution.py:20
  202.0 0.0 reduce-scatter.5.cloned.1.call-update
  202.0 26.6 %reduce-scatter.5.cloned.1.call-done = bf16[2,1,256,256]{3,2,0,1:T(8,128)(2,1)} async-done(((bf16[8,1,256,256]{3,2,0,1:T(8,128)(2,1)}), bf16[2,1,256,256]{3,2,0,1:T(8,128)(2,1)}) %reduce-scatter.5.cloned.1.call-update) | async-done | bytes 262160 | tf_op jit(solution)/shard_map/reduce_scatter | solution.py:67
  228.6 1.8 fusion.28
  (3 shorter events, 0.0 us)
Async XLA Ops:
  7.2 1.9 copy-start
  13.9 50.3 %all-to-all-start = ((bf16[2,1,8,256,256]{3,4,1,0,2:T(8,128)(2,1)}), bf16[2,1,8,256,256]{3,4,1,0,2:T(8,128)(2,1)S(1)}, u32[]{:S(2)}, u32[]{:S(2)}) async-start(bf16[2,1,8,256,256]{3,4,1,0,2:T(8,128)(2,1)} %pad_maximum_fusion), calls=%async_computation | async-start | bytes 4194304 | tf_op jit(solution)/shard_map/all_to_all | solution.py:30
  19.4 77.1 %reduce-scatter.3.cloned.1.call-start = ((), (), s32[]{:S(2)}) async-start(), calls=%async_computation.5 | async-start | bytes 1310720 | tf_op jit(solution)/shard_map/reduce_scatter | solution.py:60
  66.2 2.8 %copy-start.1 = (s32[8]{0:T(128)S(1)}, s32[8]{0:T(128)}, u32[]{:S(2)}) copy-start(s32[8]{0:T(128)} %param.13) | copy-start | bytes 100
  68.9 47.0 %all-gather.2.cloned.1.call-start = ((), (), s32[]{:S(2)}) async-start(), calls=%async_computation.6 | async-start | bytes 1310720 | tf_op jit(solution)/shard_map/all_gather | solution.py:64
  98.4 130.2 %reduce-scatter.5.cloned.1.call-start = ((), (), s32[]{:S(2)}) async-start(), calls=%async_computation.7 | async-start | bytes 1310720 | tf_op jit(solution)/shard_map/reduce_scatter | solution.py:67
Sparse Core Ops, SparseCore 0:
  69.0 27.4 reduce-scatter.2
  98.8 17.1 all-gather.1
  202.1 26.4 reduce-scatter.4
where the time goes:
time: 239 us; the launch traced here: 237 us
  waiting for transfers between devices  116 us (49%)
  blocking collectives  79.4 us (33%)
  between operations  14 us (6%)
  other arithmetic  9.37 us (4%)
  matrix products  8.46 us (4%)
  starting transfers between devices  5.64 us (2%)
  local copies, waits for them, and re-layouts  3.67 us (2%)
    all_to_all x1, blocking collectives, apply_left_layout(): lax.all_to_all(rolled, 'blk', split_axis=2, concat_axis=1, tiled=True)  51.4 us
    all_to_all x1, waiting for transfers between devices, apply_left_layout(): lax.all_to_all(rolled, 'blk', split_axis=2, concat_axis=1, tiled=True)  44.7 us
    all_to_all x1, blocking collectives, on_device(): lax.all_to_all(full_next, 'blk', split_axis=0, concat_axis=1, tiled=True)  27.9 us
    reduce_scatter x1, waiting for transfers between devices, on_device(): lax.psum_scatter(partial_value.astype(jnp.bfloat16), 'term', scatter_dime...  27.5 us
    reduce_scatter x1, waiting for transfers between devices, on_device(): lax.psum_scatter(partial_next.astype(jnp.bfloat16), 'term', scatter_dimen...  26.6 us
    all_gather x1, waiting for transfers between devices, on_device(): full_next = lax.all_gather(applied_once, 'term', axis=0, tiled=True)  17.5 us
    all_to_all x1, starting transfers between devices, apply_left_layout(): lax.all_to_all(rolled, 'blk', split_axis=2, concat_axis=1, tiled=True)  5.55 us
    dot_general x2, matrix products, right_products(): jnp.einsum('wijac,wjdc->ijad', products, right_env, preferred_element_typ...  5.34 us
  transfers between devices with their start and end apart: 4, of which 4 were waited for; matrix products, arithmetic and copies ran while one was open for 0% of the time, Pallas kernels for 0%

commit v1 on v0

v1 whole, which is shorter than its diff:
```python
import functools

import jax
import jax.numpy as jnp
from jax import lax
from jax.experimental import pallas as pl
from jax.experimental.pallas import tpu as pltpu
from jax.sharding import PartitionSpec as P

MESH = pl.DeviceIdType.MESH


def kernel(sizes, v_in, l_in, r_in, charges, dims, out1, out2,
           L, R, V, U, Y1, Y2, prod,
           x_send, x_recv, f_send, v_send, v_recv, r_send, r_recv,
           u_send, u_recv, o_send, o_recv):
    nt, nb, ny, ni, nw, tw, tile = sizes
    ns = nb
    nz = nb // ny
    half = nt // 2
    t = lax.axis_index("term")
    b = lax.axis_index("blk")

    def role_of(term):
        return (term % 2) * half + term // 2

    def device_of(role):
        return (role % half) * 2 + role // half

    def wrap(value, size):
        return (value + size) % size

    r = role_of(t)
    z, y = b // ny, b % ny

    barrier = pltpu.get_barrier_semaphore()
    for k in range(1, nt):
        pl.semaphore_signal(barrier, inc=1, device_id=((t + k) % nt, b), device_id_type=MESH)
    for k in range(1, nb):
        pl.semaphore_signal(barrier, inc=1, device_id=(t, (b + k) % nb), device_id_type=MESH)
    for s in (-1, 1):
        pl.semaphore_signal(barrier, inc=1,
                            device_id=(device_of(wrap(r + s, nt)), wrap(b - s, nb)), device_id_type=MESH)
    pl.semaphore_wait(barrier, nt - 1 + nb - 1 + 2)

    def send(src, dst, ssem, rsem, term, blk):
        pltpu.make_async_remote_copy(
            src_ref=src, dst_ref=dst, send_sem=ssem, recv_sem=rsem,
            device_id=(term, blk), device_id_type=MESH,
        ).start()

    def done(sem):
        pltpu.make_async_copy(L.at[0], L.at[0], sem).wait()

    def place(src, dst, ssem, rsem, term, blk, here):
        @pl.when(here)
        def _():
            pltpu.make_async_copy(src, dst, rsem).start()

        @pl.when(jnp.logical_not(here))
        def _():
            send(src, dst, ssem, rsem, term, blk)

    def left_target(k):
        w = t * tw + k
        i = wrap(b + w % 3 - 1, ns)
        return (i % ni) * nw + w, device_of(i // ni)

    for k in range(tw):
        slot, term = left_target(k)
        place(l_in.at[k, 0], L.at[slot], x_send.at[k], x_recv.at[slot], term, b, term == t)

    for s in (-1, 0, 1):
        i = wrap(b + s, ns)

        @pl.when(i // ni == r)
        def _():
            slot = (s + 1) * ni + i % ni
            for off in range(nb):
                to = (b + off) % nb
                src = v_in.at[0, wrap(to + s, ns)]
                if off == 0:
                    pltpu.make_async_copy(src, V.at[slot], v_recv.at[slot]).start()
                else:
                    send(src, V.at[slot], v_send.at[(s + 1) * nb + off], v_recv.at[slot], t, to)

    for k in range(tw):
        w = t * tw + k
        pltpu.make_async_copy(r_in.at[k, 0], R.at[w], r_recv.at[w]).start()
        for off in range(1, nt):
            send(r_in.at[k, 0], R.at[w], r_send.at[k * nt + off], r_recv.at[w], (t + off) % nt, b)

    def left_source(li, w):
        bs = wrap(r * ni + li - (w % 3 - 1), ns)
        return bs // ny, bs % ny

    slots = [(li, w, li * nw + w) for li in range(ni) for w in range(nw)]

    def forward(d, carry):
        for li, w, slot in slots:
            zs, ys = left_source(li, w)

            @pl.when((y == ys) & ((z - zs == d) | (zs - z == d)))
            def _():
                done(x_recv.at[slot])

                @pl.when((z >= zs) & (z < nz - 1))
                def _():
                    send(L.at[slot], L.at[slot], f_send.at[slot, 0], x_recv.at[slot], t, b + ny)

                @pl.when((z <= zs) & (z > 0))
                def _():
                    send(L.at[slot], L.at[slot], f_send.at[slot, 1], x_recv.at[slot], t, b - ny)

                for k in range(1, ny):
                    send(L.at[slot], L.at[slot], f_send.at[slot, 1 + k], x_recv.at[slot],
                         t, z * ny + (y + k) % ny)
        return carry

    lax.fori_loop(0, nz, forward, 0)

    rows = lax.broadcasted_iota(jnp.int32, (tile, tile), 0)
    columns = lax.broadcasted_iota(jnp.int32, (tile, tile), 1)

    def mask(i, j):
        near_n = jnp.abs(charges[j, 0] - charges[i, 0]) <= 1
        near_s = jnp.abs(charges[j, 1] - charges[i, 1]) <= 1
        allowed = jnp.where(near_n & near_s, 1, 0)
        return (rows < dims[i] * allowed) & (columns < dims[j])

    for s in (-1, 0, 1):
        for li in range(ni):
            slot = (s + 1) * ni + li
            done(v_recv.at[slot])
            keep = mask(wrap(r * ni + li - s, ns), wrap(b + s, ns))
            V[slot] = jnp.where(keep, V[slot].astype(jnp.float32), 0.0).astype(jnp.bfloat16)
    for w in range(nw):
        done(r_recv.at[w])

    for li, w, slot in slots:
        zs, ys = left_source(li, w)

        @pl.when(y != ys)
        def _():
            done(x_recv.at[slot])

    def image(state, li):
        total = None
        for w in range(nw):
            left = jnp.dot(L[li * nw + w], state[(w % 3) * ni + li],
                           preferred_element_type=jnp.float32).astype(jnp.bfloat16)
            part = lax.dot_general(left, R[w], (((1,), (1,)), ((), ())),
                                   preferred_element_type=jnp.float32)
            total = part if total is None else total + part
        return jnp.where(mask(r * ni + li, b), total, 0.0).astype(jnp.bfloat16)

    def deliver(n, li, src, dst):
        place(src.at[li], dst.at[li, 0], o_send.at[n * ni + li], o_recv.at[n * ni + li], r, b, r == t)

    def next_target(li, s):
        i = wrap(r * ni + li + s, ns)
        return (s + 1) * ni + i % ni, device_of(i // ni), wrap(b - s, nb)

    for li in range(ni):
        Y1[li] = image(V, li)
        for s in (-1, 1):
            slot, term, blk = next_target(li, s)
            send(Y1.at[li], U.at[slot], u_send.at[(s + 1) * ni + li], u_recv.at[slot], term, blk)
        U[ni + li] = Y1[li]
        deliver(0, li, Y1, out1)

    for s in (-1, 1):
        for li in range(ni):
            done(u_recv.at[(s + 1) * ni + li])
    for li in range(ni):
        Y2[li] = image(U, li)
        deliver(1, li, Y2, out2)

    for k in range(tw):
        slot, term = left_target(k)

        @pl.when(term != t)
        def _():
            done(x_send.at[k])

        for off in range(1, nt):
            done(r_send.at[k * nt + off])
    for s in (-1, 0, 1):
        @pl.when(wrap(b + s, ns) // ni == r)
        def _():
            for off in range(1, nb):
                done(v_send.at[(s + 1) * nb + off])
    for li, w, slot in slots:
        zs, ys = left_source(li, w)

        @pl.when(y == ys)
        def _():
            @pl.when((z >= zs) & (z < nz - 1))
            def _():
                done(f_send.at[slot, 0])

            @pl.when((z <= zs) & (z > 0))
            def _():
                done(f_send.at[slot, 1])

            for k in range(1, ny):
                done(f_send.at[slot, 1 + k])
    for s in (-1, 1):
        for li in range(ni):
            done(u_send.at[(s + 1) * ni + li])
    for n in range(2 * ni):
        done(o_recv.at[n])

        @pl.when(r != t)
        def _():
            done(o_send.at[n])


def on_device(wavefunction, left_env, right_env, charges, sector_dims):
    nt, nb = lax.axis_size("term"), lax.axis_size("blk")
    tw, tile = left_env.shape[0], left_env.shape[-1]
    ns = wavefunction.shape[1]
    assert wavefunction.shape[0] == 1 and ns == nb
    ni, nw = ns // nt, tw * nt
    ny = 1
    while 4 * ny * ny <= nb:
        ny *= 2
    sizes = (nt, nb, ny, ni, nw, tw, tile)

    def blocks(n):
        return pltpu.VMEM((n, tile, tile), jnp.bfloat16)

    dma = pltpu.SemaphoreType.DMA
    out = jax.ShapeDtypeStruct((ni, 1, tile, tile), jnp.bfloat16)
    hbm = pl.BlockSpec(memory_space=pl.ANY)
    smem = pl.BlockSpec(memory_space=pltpu.SMEM)
    return pl.pallas_call(
        functools.partial(kernel, sizes),
        out_shape=(out, out),
        in_specs=[hbm, hbm, hbm, smem, smem],
        out_specs=(hbm, hbm),
        scratch_shapes=[
            blocks(ni * nw), blocks(nw), blocks(3 * ni), blocks(3 * ni), blocks(ni), blocks(ni), blocks(1),
            dma((tw,)), dma((ni * nw,)), dma((ni * nw, 1 + ny)),
            dma((3 * nb,)), dma((3 * ni,)), dma((tw * nt,)), dma((nw,)),
            dma((3 * ni,)), dma((3 * ni,)), dma((2 * ni,)), dma((2 * ni,)),
        ],
        compiler_params=pltpu.CompilerParams(
            collective_id=0, has_side_effects=True, vmem_limit_bytes=40 * 2**20
        ),
    )(wavefunction, left_env, right_env, charges, sector_dims)


def solution(mesh):
    placed = (
        P("blk", None, None, None),
        P("term", "blk", None, None),
        P("term", "blk", None, None),
        P(),
        P(),
    )
    return jax.shard_map(
        on_device,
        mesh=mesh,
        in_specs=placed,
        out_specs=(P("term", "blk", None, None), P("term", "blk", None, None)),
        check_vma=False,
    )
```

time: 239 us -> 79 us (0.33)
  the two profiles are of different devices: /device:TPU:21 before, /device:TPU:5 now
where the time goes in v1:
time: 79 us; the launch traced here: 78.8 us
  Pallas kernels  72.8 us (92%)
  local copies, waits for them, and re-layouts  5.29 us (7%)
    pallas_call x1, Pallas kernels, on_device(): pl.pallas_call(functools.partial(kernel, sizes), out_shape=(out, out), in...  72.8 us
    unnamed x11, local copies, waits for them, and re-layouts  5.29 us

profile of v1, /device:TPU:5, one launch (start us, length us, event | category | flops | bytes accessed | tf_op | source)
XLA Modules:
  0.0 78.8 jit_solution(3221446934715433360)
XLA Ops:
  0.6 0.0 copy-start.3
  0.6 0.8 copy.7.charges
  1.4 0.0 copy-done.3
  1.4 0.0 copy-start
  1.4 1.2 %copy-done = bf16[1,8,256,256]{3,2,1,0:T(8,128)(2,1)S(1)} copy-done((bf16[1,8,256,256]{3,2,1,0:T(8,128)(2,1)S(1)}, bf16[1,8,256,256]{3,2,1,0:T(8,128)(2,1)}, u32[]{:S(2)}) %copy-start) | copy-done | bytes 1048600
  2.6 0.0 copy-start.1
  2.6 0.9 %copy-done.1 = bf16[2,1,256,256]{3,2,1,0:T(8,128)(2,1)S(1)} copy-done((bf16[2,1,256,256]{3,2,1,0:T(8,128)(2,1)S(1)}, bf16[2,1,256,256]{3,2,1,0:T(8,128)(2,1)}, u32[]{:S(2)}) %copy-start.1) | copy-done | bytes 262168
  3.6 0.0 copy-start.2
  3.6 0.9 %copy-done.2 = bf16[2,1,256,256]{3,2,1,0:T(8,128)(2,1)S(1)} copy-done((bf16[2,1,256,256]{3,2,1,0:T(8,128)(2,1)S(1)}, bf16[2,1,256,256]{3,2,1,0:T(8,128)(2,1)}, u32[]{:S(2)}) %copy-start.2) | copy-done | bytes 262168
  4.5 72.8 %shard_map.68 = (bf16[2,1,256,256]{3,2,1,0:T(8,128)(2,1)S(1)}, bf16[2,1,256,256]{3,2,1,0:T(8,128)(2,1)S(1)}) custom-call(bf16[1,8,256,256]{3,2,1,0:T(8,128)(2,1)S(1)} %copy-done, bf16[2,1,256,256]{3,2,1,0:T(8,128)(2,1)S(1)} %copy-done.1, bf16[2,1,256,256]{3,2,1,0:T(8,128)(2,1)S(1)} %copy-done.2, s32[8,2]{1,0:T(8,128)S(1)} %copy.7.charges, s32[8]{0:T(128)S(1)} %copy-done.3), custom_call_target="tpu_custom_call" | custom-call | tf_op jit(solution)/shard_map/pallas_call | solution.py:237
  77.4 0.7 copy.10
  78.1 0.7 copy.11
Async XLA Ops:
  0.6 0.8 copy-start.3
  1.4 1.2 %copy-start = (bf16[1,8,256,256]{3,2,1,0:T(8,128)(2,1)S(1)}, bf16[1,8,256,256]{3,2,1,0:T(8,128)(2,1)}, u32[]{:S(2)}) copy-start(bf16[1,8,256,256]{3,2,1,0:T(8,128)(2,1)} %v_in.1) | copy-start | bytes 3145732
  2.6 0.9 %copy-start.1 = (bf16[2,1,256,256]{3,2,1,0:T(8,128)(2,1)S(1)}, bf16[2,1,256,256]{3,2,1,0:T(8,128)(2,1)}, u32[]{:S(2)}) copy-start(bf16[2,1,256,256]{3,2,1,0:T(8,128)(2,1)} %l_in.1) | copy-start | bytes 786436
  3.6 0.9 %copy-start.2 = (bf16[2,1,256,256]{3,2,1,0:T(8,128)(2,1)S(1)}, bf16[2,1,256,256]{3,2,1,0:T(8,128)(2,1)}, u32[]{:S(2)}) copy-start(bf16[2,1,256,256]{3,2,1,0:T(8,128)(2,1)} %r_in.1) | copy-start | bytes 786436

commit v2 on v1

--- a/solution.py
+++ b/solution.py
@@ -11,7 +11,7 @@
 
 
 def kernel(sizes, v_in, l_in, r_in, charges, dims, out1, out2,
-           L, R, V, U, Y1, Y2, prod,
+           L, R, RT, V, U, Y1, Y2, prod,
            x_send, x_recv, f_send, v_send, v_recv, r_send, r_recv,
            u_send, u_recv, o_send, o_recv):
     nt, nb, ny, ni, nw, tw, tile = sizes
@@ -49,8 +49,15 @@
             device_id=(term, blk), device_id_type=MESH,
         ).start()
 
-    def done(sem):
-        pltpu.make_async_copy(L.at[0], L.at[0], sem).wait()
+    def done(sem, height=tile):
+        whole = L.at[0, pl.ds(0, height)]
+        pltpu.make_async_copy(whole, whole, sem).wait()
+
+    cuts = 2
+    part = tile // cuts
+
+    def piece(ref, k):
+        return ref.at[pl.ds(k * part, part)]
 
     def place(src, dst, ssem, rsem, term, blk, here):
         @pl.when(here)
@@ -68,9 +75,11 @@
 
     for k in range(tw):
         slot, term = left_target(k)
-        place(l_in.at[k, 0], L.at[slot], x_send.at[k], x_recv.at[slot], term, b, term == t)
-
-    for s in (-1, 0, 1):
+        for c in range(cuts):
+            place(piece(l_in.at[k, 0], c), piece(L.at[slot], c), x_send.at[k, c], x_recv.at[slot, c],
+                  term, b, term == t)
+
+    def spread(s):
         i = wrap(b + s, ns)
 
         @pl.when(i // ni == r)
@@ -84,40 +93,48 @@
                 else:
                     send(src, V.at[slot], v_send.at[(s + 1) * nb + off], v_recv.at[slot], t, to)
 
+    def left_source(li, w):
+        bs = wrap(r * ni + li - (w % 3 - 1), ns)
+        return bs // ny, bs % ny
+
+    slots = [(li, w, li * nw + w) for li in range(ni) for w in range(nw)]
+
+    def forward(d, carry):
+        for li, w, slot in slots:
+            zs, ys = left_source(li, w)
+
+            @pl.when((y == ys) & ((z - zs == d) | (zs - z == d)))
+            def _():
+                for c in range(cuts):
+                    done(x_recv.at[slot, c], part)
+                    src = piece(L.at[slot], c)
+
+                    @pl.when((z >= zs) & (z < nz - 1))
+                    def _():
+                        send(src, src, f_send.at[slot, c, 0], x_recv.at[slot, c], t, b + ny)
+
+                    @pl.when((z <= zs) & (z > 0))
+                    def _():
+                        send(src, src, f_send.at[slot, c, 1], x_recv.at[slot, c], t, b - ny)
+
+                    for k in range(1, ny):
+                        send(src, src, f_send.at[slot, c, 1 + k], x_recv.at[slot, c],
+                             t, z * ny + (y + k) % ny)
+        return carry
+
+    spread(0)
+    forward(0, 0)
+    spread(-1)
+
     for k in range(tw):
         w = t * tw + k
         pltpu.make_async_copy(r_in.at[k, 0], R.at[w], r_recv.at[w]).start()
         for off in range(1, nt):
             send(r_in.at[k, 0], R.at[w], r_send.at[k * nt + off], r_recv.at[w], (t + off) % nt, b)
 
-    def left_source(li, w):
-        bs = wrap(r * ni + li - (w % 3 - 1), ns)
-        return bs // ny, bs % ny
-
-    slots = [(li, w, li * nw + w) for li in range(ni) for w in range(nw)]
-
-    def forward(d, carry):
-        for li, w, slot in slots:
-            zs, ys = left_source(li, w)
-
-            @pl.when((y == ys) & ((z - zs == d) | (zs - z == d)))
-            def _():
-                done(x_recv.at[slot])
-
-                @pl.when((z >= zs) & (z < nz - 1))
-                def _():
-                    send(L.at[slot], L.at[slot], f_send.at[slot, 0], x_recv.at[slot], t, b + ny)
-
-                @pl.when((z <= zs) & (z > 0))
-                def _():
-                    send(L.at[slot], L.at[slot], f_send.at[slot, 1], x_recv.at[slot], t, b - ny)
-
-                for k in range(1, ny):
-                    send(L.at[slot], L.at[slot], f_send.at[slot, 1 + k], x_recv.at[slot],
-                         t, z * ny + (y + k) % ny)
-        return carry
-
-    lax.fori_loop(0, nz, forward, 0)
+    lax.fori_loop(1, 2, forward, 0)
+    spread(1)
+    lax.fori_loop(2, nz, forward, 0)
 
     rows = lax.broadcasted_iota(jnp.int32, (tile, tile), 0)
     columns = lax.broadcasted_iota(jnp.int32, (tile, tile), 1)
@@ -136,22 +153,35 @@
             V[slot] = jnp.where(keep, V[slot].astype(jnp.float32), 0.0).astype(jnp.bfloat16)
     for w in range(nw):
         done(r_recv.at[w])
+        RT[w * tile:(w + 1) * tile, :] = R[w].T
+
+    def product(state, li, w):
+        prod[li, :, w * tile:(w + 1) * tile] = jnp.dot(
+            L[li * nw + w], state[(w % 3) * ni + li], preferred_element_type=jnp.float32
+        ).astype(jnp.bfloat16)
 
     for li, w, slot in slots:
         zs, ys = left_source(li, w)
 
-        @pl.when(y != ys)
-        def _():
-            done(x_recv.at[slot])
-
-    def image(state, li):
-        total = None
-        for w in range(nw):
-            left = jnp.dot(L[li * nw + w], state[(w % 3) * ni + li],
-                           preferred_element_type=jnp.float32).astype(jnp.bfloat16)
-            part = lax.dot_general(left, R[w], (((1,), (1,)), ((), ())),
-                                   preferred_element_type=jnp.float32)
-            total = part if total is None else total + part
+        @pl.when(y == ys)
+        def _():
+            product(V, li, w)
+
+    def others(d, carry):
+        for li, w, slot in slots:
+            zs, ys = left_source(li, w)
+
+            @pl.when((y != ys) & ((z - zs == d) | (zs - z == d)))
+            def _():
+                for c in range(cuts):
+                    done(x_recv.at[slot, c], part)
+                product(V, li, w)
+        return carry
+
+    lax.fori_loop(0, nz, others, 0)
+
+    def image(li):
+        total = jnp.dot(prod[li], RT[...], preferred_element_type=jnp.float32)
         return jnp.where(mask(r * ni + li, b), total, 0.0).astype(jnp.bfloat16)
 
     def deliver(n, li, src, dst):
@@ -162,18 +192,22 @@
         return (s + 1) * ni + i % ni, device_of(i // ni), wrap(b - s, nb)
 
     for li in range(ni):
-        Y1[li] = image(V, li)
+        Y1[li] = image(li)
         for s in (-1, 1):
             slot, term, blk = next_target(li, s)
             send(Y1.at[li], U.at[slot], u_send.at[(s + 1) * ni + li], u_recv.at[slot], term, blk)
         U[ni + li] = Y1[li]
         deliver(0, li, Y1, out1)
 
-    for s in (-1, 1):
+    for s in (0, -1, 1):
         for li in range(ni):
-            done(u_recv.at[(s + 1) * ni + li])
+            if s:
+                done(u_recv.at[(s + 1) * ni + li])
+            for w in range(nw):
+                if w % 3 == s + 1:
+                    product(U, li, w)
     for li in range(ni):
-        Y2[li] = image(U, li)
+        Y2[li] = image(li)
         deliver(1, li, Y2, out2)
 
     for k in range(tw):
@@ -181,7 +215,8 @@
 
         @pl.when(term != t)
         def _():
-            done(x_send.at[k])
+            for c in range(cuts):
+                done(x_send.at[k, c], part)
 
         for off in range(1, nt):
             done(r_send.at[k * nt + off])
@@ -195,16 +230,17 @@
 
         @pl.when(y == ys)
         def _():
-            @pl.when((z >= zs) & (z < nz - 1))
-            def _():
-                done(f_send.at[slot, 0])
-
-            @pl.when((z <= zs) & (z > 0))
-            def _():
-                done(f_send.at[slot, 1])
-
-            for k in range(1, ny):
-                done(f_send.at[slot, 1 + k])
+            for c in range(cuts):
+                @pl.when((z >= zs) & (z < nz - 1))
+                def _():
+                    done(f_send.at[slot, c, 0], part)
+
+                @pl.when((z <= zs) & (z > 0))
+                def _():
+                    done(f_send.at[slot, c, 1], part)
+
+                for k in range(1, ny):
+                    done(f_send.at[slot, c, 1 + k], part)
     for s in (-1, 1):
         for li in range(ni):
             done(u_send.at[(s + 1) * ni + li])
@@ -232,21 +268,23 @@
 
     dma = pltpu.SemaphoreType.DMA
     out = jax.ShapeDtypeStruct((ni, 1, tile, tile), jnp.bfloat16)
-    hbm = pl.BlockSpec(memory_space=pl.ANY)
+    hbm = pl.BlockSpec(memory_space=pltpu.HBM)
     smem = pl.BlockSpec(memory_space=pltpu.SMEM)
+    vmem = pl.BlockSpec(memory_space=pltpu.VMEM)
     return pl.pallas_call(
         functools.partial(kernel, sizes),
         out_shape=(out, out),
         in_specs=[hbm, hbm, hbm, smem, smem],
         out_specs=(hbm, hbm),
         scratch_shapes=[
-            blocks(ni * nw), blocks(nw), blocks(3 * ni), blocks(3 * ni), blocks(ni), blocks(ni), blocks(1),
-            dma((tw,)), dma((ni * nw,)), dma((ni * nw, 1 + ny)),
+            blocks(ni * nw), blocks(nw), pltpu.VMEM((nw * tile, tile), jnp.bfloat16), blocks(3 * ni), blocks(3 * ni), blocks(ni), blocks(ni),
+            pltpu.VMEM((ni, tile, nw * tile), jnp.bfloat16),
+            dma((tw, 2)), dma((ni * nw, 2)), dma((ni * nw, 2, 1 + ny)),
             dma((3 * nb,)), dma((3 * ni,)), dma((tw * nt,)), dma((nw,)),
             dma((3 * ni,)), dma((3 * ni,)), dma((2 * ni,)), dma((2 * ni,)),
         ],
         compiler_params=pltpu.CompilerParams(
-            collective_id=0, has_side_effects=True, vmem_limit_bytes=40 * 2**20
+            collective_id=0, has_side_effects=True, vmem_limit_bytes=60 * 2**20
         ),
     )(wavefunction, left_env, right_env, charges, sector_dims)
 

time: 79 us -> 72 us (0.911)
  the two profiles are of different devices: /device:TPU:5 before, /device:TPU:21 now
where the time goes in v2:
time: 72 us; the launch traced here: 71.8 us
  Pallas kernels  67.3 us (93%)
  local copies, waits for them, and re-layouts  3.76 us (5%)
    pallas_call x1, Pallas kernels, on_device(): pl.pallas_call(functools.partial(kernel, sizes), out_shape=(out, out), in...  67.3 us
    unnamed x5, local copies, waits for them, and re-layouts  3.76 us

profile of v2, /device:TPU:21, one launch (start us, length us, event | category | flops | bytes accessed | tf_op | source)
XLA Modules:
  0.0 71.8 jit_solution(18115692513504656402)
XLA Ops:
  0.6 1.3 %copy.7.charges = s32[8,2]{1,0:T(8,128)} copy(s32[8,2]{0,1:T(2,128)} %param.8) | data formatting | bytes 128 | tf_op args[3]
  2.0 67.3 %shard_map.68 = (bf16[2,1,256,256]{3,2,1,0:T(8,128)(2,1)}, bf16[2,1,256,256]{3,2,1,0:T(8,128)(2,1)}) custom-call(bf16[1,8,256,256]{3,2,1,0:T(8,128)(2,1)} %v_in.1, bf16[2,1,256,256]{3,2,1,0:T(8,128)(2,1)} %l_in.1, bf16[2,1,256,256]{3,2,1,0:T(8,128)(2,1)} %r_in.1, s32[8,2]{1,0:T(8,128)} %copy.7.charges, s32[8]{0:T(128)} %dims.1), custom_call_target="tpu_custom_call" | custom-call | tf_op jit(solution)/shard_map/pallas_call | solution.py:274
  69.3 0.0 copy-start
  69.3 1.7 %copy.10 = bf16[2,1,256,256]{3,2,1,0:T(8,128)(2,1)} copy(bf16[2,1,256,256]{3,2,1,0:T(8,128)(2,1)} %get-tuple-element.4) | data formatting | bytes 524288
  71.1 0.0 copy-done
  71.1 0.7 copy.11
Async XLA Ops:
  69.3 1.7 %copy-start = (bf16[2,1,256,256]{3,2,1,0:T(8,128)(2,1)S(1)}, bf16[2,1,256,256]{3,2,1,0:T(8,128)(2,1)}, u32[]{:S(2)}) copy-start(bf16[2,1,256,256]{3,2,1,0:T(8,128)(2,1)} %get-tuple-element.5) | copy-start | bytes 786436

commit v3 on v2

--- a/solution.py
+++ b/solution.py
@@ -126,14 +126,15 @@
     forward(0, 0)
     spread(-1)
 
+    lax.fori_loop(1, 2, forward, 0)
+    spread(1)
+
     for k in range(tw):
         w = t * tw + k
         pltpu.make_async_copy(r_in.at[k, 0], R.at[w], r_recv.at[w]).start()
         for off in range(1, nt):
             send(r_in.at[k, 0], R.at[w], r_send.at[k * nt + off], r_recv.at[w], (t + off) % nt, b)
 
-    lax.fori_loop(1, 2, forward, 0)
-    spread(1)
     lax.fori_loop(2, nz, forward, 0)
 
     rows = lax.broadcasted_iota(jnp.int32, (tile, tile), 0)

time: 72 us -> 72 us (level)
  no operation moved by 1% of the time
where the time goes in v3:
time: 72 us; the launch traced here: 71.8 us
  Pallas kernels  67.3 us (93%)
  local copies, waits for them, and re-layouts  3.76 us (5%)
    pallas_call x1, Pallas kernels, on_device(): pl.pallas_call(functools.partial(kernel, sizes), out_shape=(out, out), in...  67.3 us
    unnamed x5, local copies, waits for them, and re-layouts  3.76 us

profile of v3, /device:TPU:21, one launch (start us, length us, event | category | flops | bytes accessed | tf_op | source)
XLA Modules:
  0.0 71.8 jit_solution(6685984151762591871)
XLA Ops:
  0.6 1.3 %copy.7.charges = s32[8,2]{1,0:T(8,128)} copy(s32[8,2]{0,1:T(2,128)} %param.8) | data formatting | bytes 128 | tf_op args[3]
  2.0 67.3 %shard_map.68 = (bf16[2,1,256,256]{3,2,1,0:T(8,128)(2,1)}, bf16[2,1,256,256]{3,2,1,0:T(8,128)(2,1)}) custom-call(bf16[1,8,256,256]{3,2,1,0:T(8,128)(2,1)} %v_in.1, bf16[2,1,256,256]{3,2,1,0:T(8,128)(2,1)} %l_in.1, bf16[2,1,256,256]{3,2,1,0:T(8,128)(2,1)} %r_in.1, s32[8,2]{1,0:T(8,128)} %copy.7.charges, s32[8]{0:T(128)} %dims.1), custom_call_target="tpu_custom_call" | custom-call | tf_op jit(solution)/shard_map/pallas_call | solution.py:275
  69.3 0.0 copy-start
  69.3 1.7 %copy.10 = bf16[2,1,256,256]{3,2,1,0:T(8,128)(2,1)} copy(bf16[2,1,256,256]{3,2,1,0:T(8,128)(2,1)} %get-tuple-element.4) | data formatting | bytes 524288
  71.0 0.0 copy-done
  71.0 0.7 copy.11
Async XLA Ops:
  69.3 1.7 %copy-start = (bf16[2,1,256,256]{3,2,1,0:T(8,128)(2,1)S(1)}, bf16[2,1,256,256]{3,2,1,0:T(8,128)(2,1)}, u32[]{:S(2)}) copy-start(bf16[2,1,256,256]{3,2,1,0:T(8,128)(2,1)} %get-tuple-element.5) | copy-start | bytes 786436
